TPU v7x, 128 devices: a whole 4x4x4 slice. The times are simulated.
128 devices in a mesh: dp: 2 (over x_hi), blk: 64 (over x_lo, y, z, core).
Axes of the slice: x: 4 (x_hi: 2, x_lo: 2; x = x_hi * 2 + x_lo), y: 4, z: 4, core: 2. Of those that a mesh axis runs over, the one named last changes fastest.
Arguments:
- queries: bfloat16 [32768, 2048], P(('dp', 'blk')), parts along dimension 0, may hold values from -8 to 8
- key_rows: bfloat16 [32768, 2048], P(('dp', 'blk')), parts along dimension 0, may hold values from -8 to 8
- value_rows: bfloat16 [32768, 2048], P(('dp', 'blk')), parts along dimension 0, may hold values from -6 to 6
- out_grad: bfloat16 [32768, 2048], P(('dp', 'blk')), parts along dimension 0, may hold values from -6 to 6
- doc_lengths: int32 [32], P('dp'), parts along dimension 0, may hold values from 1 to 1536, 16384 in all
Outputs:
- attended: bfloat16 [32768, 2048], P(('dp', 'blk')), parts along dimension 0
- query_grad: bfloat16 [32768, 2048], P(('dp', 'blk')), parts along dimension 0
- key_grad: bfloat16 [32768, 2048], P(('dp', 'blk')), parts along dimension 0
- value_grad: bfloat16 [32768, 2048], P(('dp', 'blk')), parts along dimension 0
There are 2 independent parts, one for each index of `dp`. A program takes and returns all parts, laid end to end along the dimension named above; each array names one. Nothing has to cross between parts.
Inputs may be any that keep to these rules, and one draw needn't show every extreme that they name: `doc_lengths`: the lengths sum to 16384; the longest document has exactly 1536 tokens.
All inputs are finite; a program needn't handle non-finite values.
Results may differ from a plain program's by a relative error of at most 0.011.
Values may be sent and summed in bfloat16 or wider, within the bound.
A program may use at most 192 MiB of HBM per device.

v0:
```python
import math

import jax
import jax.numpy as jnp
from jax import lax
from jax.sharding import PartitionSpec as P

HEAD_DIM = 128
REACH = 6


NEG_FILL = -1e30


def from_behind(block, axis, distance):
    devices = range(lax.axis_size(axis))
    route = [(i - distance, i) for i in devices if i - distance in devices]
    return lax.ppermute(block, axis, route)


def document_index(doc_lengths, positions):
    doc_ends = jnp.cumsum(doc_lengths)
    return jnp.sum((doc_ends[None, :] <= positions[:, None]).astype(jnp.int32), axis=1)


def allowed_pairs(query_pos, key_pos, doc_lengths):
    same_doc = (
        document_index(doc_lengths, query_pos)[:, None]
        == document_index(doc_lengths, key_pos)[None, :]
    )
    return same_doc & (key_pos[None, :] <= query_pos[:, None]) & (key_pos[None, :] >= 0)


def split_heads(matrix):
    return matrix.reshape(matrix.shape[0], matrix.shape[1] // HEAD_DIM, HEAD_DIM).transpose(1, 0, 2)


def merge_heads(matrix):
    head_count, row_count, head_size = matrix.shape
    return matrix.transpose(1, 0, 2).reshape(row_count, head_count * head_size)


def masked_scores(query_head, key_head, allowed):
    scores = jnp.einsum("td,kd->tk", query_head, key_head, preferred_element_type=jnp.float32) * (
        1.0 / math.sqrt(HEAD_DIM)
    )
    return jnp.where(allowed, scores, NEG_FILL)


def forward_head(query_head, key_head, value_head, allowed):
    scores = masked_scores(query_head, key_head, allowed)
    row_max = jnp.max(scores, axis=1, keepdims=True)
    log_total = row_max + jnp.log(jnp.sum(jnp.exp(scores - row_max), axis=1, keepdims=True))
    weights = jnp.where(allowed, jnp.exp(scores - log_total), 0.0).astype(jnp.bfloat16)
    return (jnp.dot(weights, value_head, preferred_element_type=jnp.float32), log_total[:, 0])


def backward_head(query_head, grad_head, log_total, row_delta, key_head, value_head, allowed):
    scores = masked_scores(query_head, key_head, allowed)
    weights = jnp.where(allowed, jnp.exp(scores - log_total[:, None]), 0.0)
    weight_grads = jnp.einsum(
        "td,kd->tk", grad_head, value_head, preferred_element_type=jnp.float32
    )
    score_low = (
        weights * (weight_grads - row_delta[:, None]) * (1.0 / math.sqrt(HEAD_DIM))
    ).astype(jnp.bfloat16)
    query_part = jnp.dot(score_low, key_head, preferred_element_type=jnp.float32)
    key_part = jnp.einsum("tk,td->kd", score_low, query_head, preferred_element_type=jnp.float32)
    value_part = jnp.einsum(
        "tk,td->kd", weights.astype(jnp.bfloat16), grad_head, preferred_element_type=jnp.float32
    )
    return (query_part, key_part, value_part)


def run_backward(query_heads, grad_heads, log_total, row_delta, key_heads, value_heads, allowed):

    def one_head(head_items):
        return backward_head(
            head_items[0],
            head_items[1],
            head_items[2],
            head_items[3],
            head_items[4],
            head_items[5],
            allowed,
        )

    return lax.map(
        one_head, (query_heads, grad_heads, log_total, row_delta, key_heads, value_heads)
    )


def on_device(queries, key_rows, value_rows, out_grad, doc_lengths):
    shard_rows = queries.shape[0]
    device = lax.axis_index("blk")
    first_row = device * shard_rows
    query_pos = first_row + jnp.arange(shard_rows, dtype=jnp.int32)
    remote = [(key_rows, value_rows)]
    carried_keys, carried_values = (key_rows, value_rows)
    for offset in range(1, REACH + 1):
        carried_keys, carried_values = from_behind((carried_keys, carried_values), "blk", 1)
        remote.append((carried_keys, carried_values))
    ordered = remote[::-1]
    key_window = jnp.concatenate([shard_pair[0] for shard_pair in ordered], axis=0)
    value_window = jnp.concatenate([shard_pair[1] for shard_pair in ordered], axis=0)
    key_pos = first_row - REACH * shard_rows + jnp.arange((REACH + 1) * shard_rows, dtype=jnp.int32)
    allowed = allowed_pairs(query_pos, key_pos, doc_lengths)
    query_heads = split_heads(queries)
    key_heads = split_heads(key_window)
    value_heads = split_heads(value_window)

    def forward_one(head_items):
        return forward_head(head_items[0], head_items[1], head_items[2], allowed)

    head_out, log_total = lax.map(forward_one, (query_heads, key_heads, value_heads))
    attended = merge_heads(head_out).astype(jnp.bfloat16)
    grad_heads = split_heads(out_grad)
    row_delta = jnp.sum(
        grad_heads.astype(jnp.float32) * split_heads(attended).astype(jnp.float32), axis=2
    )
    query_part, key_part, value_part = run_backward(
        query_heads, grad_heads, log_total, row_delta, key_heads, value_heads, allowed
    )
    query_total = merge_heads(query_part)
    key_window_grads = merge_heads(key_part)
    value_window_grads = merge_heads(value_part)
    key_total = key_window_grads[REACH * shard_rows :]
    value_total = value_window_grads[REACH * shard_rows :]
    for offset in range(1, REACH + 1):
        row_start = (REACH - offset) * shard_rows
        sent_keys, sent_values = from_behind(
            (
                key_window_grads[row_start : row_start + shard_rows],
                value_window_grads[row_start : row_start + shard_rows],
            ),
            "blk",
            -offset,
        )
        key_total = key_total + sent_keys
        value_total = value_total + sent_values
    return (
        attended,
        query_total.astype(jnp.bfloat16),
        key_total.astype(jnp.bfloat16),
        value_total.astype(jnp.bfloat16),
    )


def solution(mesh):
    in_specs = (
        P(("dp", "blk"), None),
        P(("dp", "blk"), None),
        P(("dp", "blk"), None),
        P(("dp", "blk"), None),
        P("dp"),
    )
    out_specs = (
        P(("dp", "blk"), None),
        P(("dp", "blk"), None),
        P(("dp", "blk"), None),
        P(("dp", "blk"), None),
    )
    return jax.shard_map(
        on_device, mesh=mesh, in_specs=in_specs, out_specs=out_specs, check_vma=False
    )
```

profile of v0, /device:TPU:56, one launch (start us, length us, event | category | flops | bytes accessed | tf_op | source)
XLA Modules:
  0.0 1080.6 jit_solution(14062014937051464780)
XLA Ops:
  4.7 3.9 collective-permute-start.6
  8.6 9.8 collective-permute-done
  20.4 9.2 collective-permute-done.6
  32.5 8.3 collective-permute-done.1
  42.7 9.3 collective-permute-done.7
  54.9 8.3 collective-permute-done.2
  65.2 9.3 collective-permute-done.8
  77.4 8.3 collective-permute-done.3
  87.7 9.4 collective-permute-done.9
  99.0 9.3 collective-permute-done.4
  112.0 2.3 copy.57
  114.3 2.3 copy.63
  116.8 2.8 collective-permute-done.10
  121.5 9.3 collective-permute-done.5
  130.8 2.3 constant_dynamic-update-slice_fusion.6
  133.1 2.5 constant_dynamic-update-slice_fusion.5
  139.0 2.3 constant_dynamic-update-slice_fusion.1
  142.4 9.9 copy.64
  152.3 2.3 constant_dynamic-update-slice_fusion.13
  154.7 2.4 constant_dynamic-update-slice_fusion.12
  157.1 2.4 constant_dynamic-update-slice_fusion.11
  164.1 10.1 copy.65
  174.2 66.9 %while.28 = (s32[]{:T(128)}, bf16[16,256,128]{1,2,0:T(8,128)(2,1)S(1)}, f32[16,256]{1,0:T(8,128)S(1)}, bf16[16,256,128]{2,1,0:T(8,128)(2,1)}, bf16[16,1792,128]{...) while((s32[]{:T(128)}, ...), condition=%wide.region_6.7_spmd.clone, body=%wide.region_3.6_spmd.clone.sunk | while | flops 242220800 | bytes 6669193 | solution.py:115
  241.4 145.6 %while.29 = (s32[]{:T(128)}, bf16[16,256,128]{2,1,0:T(8,128)(2,1)}, f32[16,1792,128]{2,1,0:T(8,128)}, f32[16,1792,128]{2,1,0:T(8,128)}, bf16[16,256,128]{2,1,0:T...) while((s32[]{:T(128)}, bf16[16,256,128]{2,1,0:T(8,128)(2,1)}, ...), condition=%wide.region_9.10_spmd.clone, body=%wide.region_8.9_spmd.clone.sunk | while | flops 593166336 | bytes 11891617 | solution.py:88
  266.5 2.2 fusion.102
  275.6 2.2 fusion.102
  284.7 2.3 fusion.102
  311.9 2.3 fusion.102
  321.1 2.3 fusion.102
  330.3 2.2 fusion.102
  357.5 2.3 fusion.102
  387.0 10.0 slice_bitcast_fusion.6
  397.0 3.3 copy.127
  403.8 4.1 collective-permute-start.19
  416.6 3.1 collective-permute-start.20
  419.6 4.3 collective-permute-start.21
  426.0 10.6 slice_bitcast_fusion.13
  438.6 23.9 %collective-permute-done.18 = f32[256,2048]{1,0:T(8,128)} collective-permute-done((f32[256,2048]{1,0:T(8,128)}, f32[256,2048]{1,0:T(8,128)}, u32[]{:S(2)}, u32[]{:S(2)}) %collective-permute-start.18) | collective-permute-done | bytes 2097184 | tf_op jit(solution)/shard_map/ppermute | solution.py:18
  464.4 87.0 %collective-permute-done.19 = f32[256,2048]{1,0:T(8,128)} collective-permute-done((f32[256,2048]{1,0:T(8,128)}, f32[256,2048]{1,0:T(8,128)}, u32[]{:S(2)}, u32[]{:S(2)}) %collective-permute-start.19) | collective-permute-done | bytes 2097184 | tf_op jit(solution)/shard_map/ppermute | solution.py:18
  564.3 83.5 %collective-permute-start.13 = (f32[256,2048]{1,0:T(8,128)}, f32[256,2048]{1,0:T(8,128)}, u32[]{:S(2)}, u32[]{:S(2)}) collective-permute-start(f32[256,2048]{1,0:T(8,128)} %bitcast.172), channel_id=1, source_target_pairs={{2,0},{3,1},{4,2},{5,3},{6,4},{7,5},{8,6},{9,7},{10,8},{11,9},{12,... | collective-permute-start | bytes 6291464 | tf_op jit(solution)/shard_map/ppermute | solution.py:18
  647.9 7.0 collective-permute-start.14
  654.9 16.3 %collective-permute-done.22 = f32[256,2048]{1,0:T(8,128)} collective-permute-done((f32[256,2048]{1,0:T(8,128)}, f32[256,2048]{1,0:T(8,128)}, u32[]{:S(2)}, u32[]{:S(2)}) %collective-permute-start.22) | collective-permute-done | bytes 2097184 | tf_op jit(solution)/shard_map/ppermute | solution.py:18
  673.1 127.5 %collective-permute-done.23 = f32[256,2048]{1,0:T(8,128)} collective-permute-done((f32[256,2048]{1,0:T(8,128)S(1)}, f32[256,2048]{1,0:T(8,128)}, u32[]{:S(2)}, u32[]{:S(2)}) %collective-permute-start.23) | collective-permute-done | bytes 2097184 | tf_op jit(solution)/shard_map/ppermute | solution.py:18
  805.9 2.4 copy_bitcast_fusion.12
  808.3 7.0 fusion.57
  815.3 33.7 %collective-permute-done.16 = f32[256,2048]{1,0:T(8,128)} collective-permute-done((f32[256,2048]{1,0:T(8,128)}, f32[256,2048]{1,0:T(8,128)}, u32[]{:S(2)}, u32[]{:S(2)}) %collective-permute-start.16) | collective-permute-done | bytes 2097184 | tf_op jit(solution)/shard_map/ppermute | solution.py:18
  849.0 224.7 %collective-permute-done.17 = f32[256,2048]{1,0:T(8,128)} collective-permute-done((f32[256,2048]{1,0:T(8,128)}, f32[256,2048]{1,0:T(8,128)}, u32[]{:S(2)}, u32[]{:S(2)}) %collective-permute-start.17) | collective-permute-done | bytes 2097184 | tf_op jit(solution)/shard_map/ppermute | solution.py:18
  1073.6 6.9 fusion.63
  (285 shorter events, 271.5 us)
Async XLA Ops:
  0.6 3.5 copy-start.13
  0.6 109.7 %copy-start.26 = (s32[16]{0:T(128)S(1)}, s32[16]{0:T(128)}, u32[]{:S(2)}) copy-start(s32[16]{0:T(128)} %param.13) | copy-start | bytes 196
  2.2 16.2 %collective-permute-start = (bf16[256,2048]{0,1:T(8,128)(2,1)S(1)}, bf16[256,2048]{0,1:T(8,128)(2,1)}, u32[]{:S(2)}, u32[]{:S(2)}) collective-permute-start(bf16[256,2048]{0,1:T(8,128)(2,1)S(1)} %copy.58), channel_id=1, source_target_pairs={{0,1},{1,2},{2,3},{3,4},{4,5},{5,6},{6,7},{7,8},{8,9},{9,10},{10,1... | collective-permute-start | bytes 3145736 | tf_op jit(solution)/shard_map/ppermute | solution.py:18
  4.7 24.9 %collective-permute-start.6 = (bf16[256,2048]{0,1:T(8,128)(2,1)S(1)}, bf16[256,2048]{0,1:T(8,128)(2,1)S(1)}, u32[]{:S(2)}, u32[]{:S(2)}) collective-permute-start(bf16[256,2048]{0,1:T(8,128)(2,1)S(1)} %copy.60), channel_id=1, source_target_pairs={{0,1},{1,2},{2,3},{3,4},{4,5},{5,6},{6,7},{7,8},{8,9},{9,10},{10,1... | collective-permute-start | bytes 3145736 | tf_op jit(solution)/shard_map/ppermute | solution.py:18
  18.4 22.4 %collective-permute-start.1 = (bf16[256,2048]{0,1:T(8,128)(2,1)}, bf16[256,2048]{0,1:T(8,128)(2,1)S(1)}, u32[]{:S(2)}, u32[]{:S(2)}) collective-permute-start(bf16[256,2048]{0,1:T(8,128)(2,1)} %collective-permute-done), channel_id=1, source_target_pairs={{0,1},{1,2},{2,3},{3,4},{4,5},{5,6},{6,7},{7,8},{8,9},{9,10},{10,1... | collective-permute-start | bytes 3145736 | tf_op jit(solution)/shard_map/ppermute | solution.py:18
  30.6 21.5 %collective-permute-start.7 = (bf16[256,2048]{0,1:T(8,128)(2,1)S(1)}, bf16[256,2048]{0,1:T(8,128)(2,1)S(1)}, u32[]{:S(2)}, u32[]{:S(2)}) collective-permute-start(bf16[256,2048]{0,1:T(8,128)(2,1)S(1)} %collective-permute-done.6), channel_id=1, source_target_pairs={{0,1},{1,2},{2,3},{3,4},{4,5},{5,6},{6,7},{7,8},{8,9},{9,10},{10,1... | collective-permute-start | bytes 3145736 | tf_op jit(solution)/shard_map/ppermute | solution.py:18
  40.8 56.3 %copy-start.20 = (bf16[256,2048]{0,1:T(8,128)(2,1)}, bf16[256,2048]{0,1:T(8,128)(2,1)S(1)}, u32[]{:S(2)}) copy-start(bf16[256,2048]{0,1:T(8,128)(2,1)S(1)} %collective-permute-done.1) | copy-start | bytes 3145732
  40.8 22.5 %collective-permute-start.2 = (bf16[256,2048]{0,1:T(8,128)(2,1)S(1)}, bf16[256,2048]{0,1:T(8,128)(2,1)S(1)}, u32[]{:S(2)}, u32[]{:S(2)}) collective-permute-start(bf16[256,2048]{0,1:T(8,128)(2,1)S(1)} %collective-permute-done.1), channel_id=1, source_target_pairs={{0,1},{1,2},{2,3},{3,4},{4,5},{5,6},{6,7},{7,8},{8,9},{9,10},{10,1... | collective-permute-start | bytes 3145736 | tf_op jit(solution)/shard_map/ppermute | solution.py:18
  53.0 21.5 %collective-permute-start.8 = (bf16[256,2048]{0,1:T(8,128)(2,1)S(1)}, bf16[256,2048]{0,1:T(8,128)(2,1)S(1)}, u32[]{:S(2)}, u32[]{:S(2)}) collective-permute-start(bf16[256,2048]{0,1:T(8,128)(2,1)S(1)} %collective-permute-done.7), channel_id=1, source_target_pairs={{0,1},{1,2},{2,3},{3,4},{4,5},{5,6},{6,7},{7,8},{8,9},{9,10},{10,1... | collective-permute-start | bytes 3145736 | tf_op jit(solution)/shard_map/ppermute | solution.py:18
  63.3 35.7 %copy-start.22 = (bf16[256,2048]{0,1:T(8,128)(2,1)}, bf16[256,2048]{0,1:T(8,128)(2,1)S(1)}, u32[]{:S(2)}) copy-start(bf16[256,2048]{0,1:T(8,128)(2,1)S(1)} %collective-permute-done.2) | copy-start | bytes 3145732
  63.3 22.5 %collective-permute-start.3 = (bf16[256,2048]{0,1:T(8,128)(2,1)S(1)}, bf16[256,2048]{0,1:T(8,128)(2,1)S(1)}, u32[]{:S(2)}, u32[]{:S(2)}) collective-permute-start(bf16[256,2048]{0,1:T(8,128)(2,1)S(1)} %collective-permute-done.2), channel_id=1, source_target_pairs={{0,1},{1,2},{2,3},{3,4},{4,5},{5,6},{6,7},{7,8},{8,9},{9,10},{10,1... | collective-permute-start | bytes 3145736 | tf_op jit(solution)/shard_map/ppermute | solution.py:18
  75.5 21.6 %collective-permute-start.9 = (bf16[256,2048]{0,1:T(8,128)(2,1)S(1)}, bf16[256,2048]{0,1:T(8,128)(2,1)}, u32[]{:S(2)}, u32[]{:S(2)}) collective-permute-start(bf16[256,2048]{0,1:T(8,128)(2,1)S(1)} %collective-permute-done.8), channel_id=1, source_target_pairs={{0,1},{1,2},{2,3},{3,4},{4,5},{5,6},{6,7},{7,8},{8,9},{9,10},{10,1... | collective-permute-start | bytes 3145736 | tf_op jit(solution)/shard_map/ppermute | solution.py:18
  85.8 22.6 %copy-start.24 = (bf16[256,2048]{0,1:T(8,128)(2,1)}, bf16[256,2048]{0,1:T(8,128)(2,1)S(1)}, u32[]{:S(2)}) copy-start(bf16[256,2048]{0,1:T(8,128)(2,1)S(1)} %collective-permute-done.3) | copy-start | bytes 3145732
  85.8 22.6 %collective-permute-start.4 = (bf16[256,2048]{0,1:T(8,128)(2,1)S(1)}, bf16[256,2048]{0,1:T(8,128)(2,1)}, u32[]{:S(2)}, u32[]{:S(2)}) collective-permute-start(bf16[256,2048]{0,1:T(8,128)(2,1)S(1)} %collective-permute-done.3), channel_id=1, source_target_pairs={{0,1},{1,2},{2,3},{3,4},{4,5},{5,6},{6,7},{7,8},{8,9},{9,10},{10,1... | collective-permute-start | bytes 3145736 | tf_op jit(solution)/shard_map/ppermute | solution.py:18
  97.1 22.5 %collective-permute-start.10 = (bf16[256,2048]{0,1:T(8,128)(2,1)}, bf16[256,2048]{0,1:T(8,128)(2,1)}, u32[]{:S(2)}, u32[]{:S(2)}) collective-permute-start(bf16[256,2048]{0,1:T(8,128)(2,1)} %collective-permute-done.9), channel_id=1, source_target_pairs={{0,1},{1,2},{2,3},{3,4},{4,5},{5,6},{6,7},{7,8},{8,9},{9,10},{10,1... | collective-permute-start | bytes 3145736 | tf_op jit(solution)/shard_map/ppermute | solution.py:18
  108.3 22.5 %collective-permute-start.5 = (bf16[256,2048]{0,1:T(8,128)(2,1)}, bf16[256,2048]{0,1:T(8,128)(2,1)}, u32[]{:S(2)}, u32[]{:S(2)}) collective-permute-start(bf16[256,2048]{0,1:T(8,128)(2,1)} %collective-permute-done.4), channel_id=1, source_target_pairs={{0,1},{1,2},{2,3},{3,4},{4,5},{5,6},{6,7},{7,8},{8,9},{9,10},{10,1... | collective-permute-start | bytes 3145736 | tf_op jit(solution)/shard_map/ppermute | solution.py:18
  116.8 18.8 %copy-start.25 = (bf16[256,2048]{0,1:T(8,128)(2,1)S(1)}, bf16[256,2048]{0,1:T(8,128)(2,1)}, u32[]{:S(2)}) copy-start(bf16[256,2048]{0,1:T(8,128)(2,1)} %copy-done.24) | copy-start | bytes 3145732
  119.6 32.8 %collective-permute-start.11 = (bf16[256,2048]{0,1:T(8,128)(2,1)}, bf16[256,2048]{0,1:T(8,128)(2,1)}, u32[]{:S(2)}, u32[]{:S(2)}) collective-permute-start(bf16[256,2048]{0,1:T(8,128)(2,1)} %collective-permute-done.10), channel_id=1, source_target_pairs={{0,1},{1,2},{2,3},{3,4},{4,5},{5,6},{6,7},{7,8},{8,9},{9,10},{10,1... | collective-permute-start | bytes 3145736 | tf_op jit(solution)/shard_map/ppermute | solution.py:18
  133.1 3.6 copy-start.23
  135.6 2.3 copy-start.21
  154.7 4.8 copy-start.19
  157.1 3.5 copy-start.17
  159.5 2.3 copy-start.15
  164.1 10.1 copy-start.11
  397.0 5.2 copy-start.10
  400.3 62.2 %collective-permute-start.18 = (f32[256,2048]{1,0:T(8,128)}, f32[256,2048]{1,0:T(8,128)}, u32[]{:S(2)}, u32[]{:S(2)}) collective-permute-start(f32[256,2048]{1,0:T(8,128)} %bitcast.167), channel_id=1, source_target_pairs={{1,0},{2,1},{3,2},{4,3},{5,4},{6,5},{7,6},{8,7},{9,8},{10,9},{11,1... | collective-permute-start | bytes 6291464 | tf_op jit(solution)/shard_map/ppermute | solution.py:18
  402.3 5.7 copy-start.9
  403.8 147.6 %collective-permute-start.19 = (f32[256,2048]{1,0:T(8,128)}, f32[256,2048]{1,0:T(8,128)}, u32[]{:S(2)}, u32[]{:S(2)}) collective-permute-start(f32[256,2048]{1,0:T(8,128)} %bitcast.166), channel_id=1, source_target_pairs={{2,0},{3,1},{4,2},{5,3},{6,4},{7,5},{8,6},{9,7},{10,8},{11,9},{12,... | collective-permute-start | bytes 6291464 | tf_op jit(solution)/shard_map/ppermute | solution.py:18
  408.0 2.3 copy-start.8
  410.3 2.3 copy-start.7
  412.7 2.3 copy-start.6
  416.6 147.8 %collective-permute-start.20 = (f32[256,2048]{1,0:T(8,128)}, f32[256,2048]{1,0:T(8,128)}, u32[]{:S(2)}, u32[]{:S(2)}) collective-permute-start(f32[256,2048]{1,0:T(8,128)} %bitcast.165), channel_id=1, source_target_pairs={{3,0},{4,1},{5,2},{6,3},{7,4},{8,5},{9,6},{10,7},{11,8},{12,9},{13... | collective-permute-start | bytes 6291464 | tf_op jit(solution)/shard_map/ppermute | solution.py:18
  419.6 228.3 %collective-permute-start.21 = (f32[256,2048]{1,0:T(8,128)}, f32[256,2048]{1,0:T(8,128)}, u32[]{:S(2)}, u32[]{:S(2)}) collective-permute-start(f32[256,2048]{1,0:T(8,128)} %bitcast.164), channel_id=1, source_target_pairs={{4,0},{5,1},{6,2},{7,3},{8,4},{9,5},{10,6},{11,7},{12,8},{13,9},{1... | collective-permute-start | bytes 6291464 | tf_op jit(solution)/shard_map/ppermute | solution.py:18
  423.9 247.3 %collective-permute-start.22 = (f32[256,2048]{1,0:T(8,128)}, f32[256,2048]{1,0:T(8,128)}, u32[]{:S(2)}, u32[]{:S(2)}) collective-permute-start(f32[256,2048]{1,0:T(8,128)} %bitcast.163), channel_id=1, source_target_pairs={{5,0},{6,1},{7,2},{8,3},{9,4},{10,5},{11,6},{12,7},{13,8},{14,9},{... | collective-permute-start | bytes 6291464 | tf_op jit(solution)/shard_map/ppermute | solution.py:18
  436.6 25.9 %copy-start.12 = (f32[16,32,8,128]{3,2,0,1:T(8,128)S(1)}, f32[16,32,8,128]{3,2,0,1:T(8,128)}, u32[]{:S(2)}) copy-start(f32[16,32,8,128]{3,2,0,1:T(8,128)} %copy.122) | copy-start | bytes 6291460
  436.6 116.7 %copy-start.5 = (f32[16,32,8,128]{3,2,1,0:T(8,128)S(1)}, f32[16,32,8,128]{3,2,1,0:T(8,128)}, u32[]{:S(2)}) copy-start(f32[16,32,8,128]{3,2,1,0:T(8,128)} %get-tuple-element.296) | copy-start | bytes 6291460
  462.5 338.1 %collective-permute-start.23 = (f32[256,2048]{1,0:T(8,128)S(1)}, f32[256,2048]{1,0:T(8,128)}, u32[]{:S(2)}, u32[]{:S(2)}) collective-permute-start(f32[256,2048]{1,0:T(8,128)S(1)} %bitcast.217), channel_id=1, source_target_pairs={{6,0},{7,1},{8,2},{9,3},{10,4},{11,5},{12,6},{13,7},{14,8},{15,9},... | collective-permute-start | bytes 6291464 | tf_op jit(solution)/shard_map/ppermute | solution.py:18
  551.5 251.1 %collective-permute-start.12 = (f32[256,2048]{1,0:T(8,128)S(1)}, f32[256,2048]{1,0:T(8,128)}, u32[]{:S(2)}, u32[]{:S(2)}) collective-permute-start(f32[256,2048]{1,0:T(8,128)S(1)} %bitcast.218), channel_id=1, source_target_pairs={{1,0},{2,1},{3,2},{4,3},{5,4},{6,5},{7,6},{8,7},{9,8},{10,9},{11,1... | collective-permute-start | bytes 6291464 | tf_op jit(solution)/shard_map/ppermute | solution.py:18
  553.4 2.3 copy-start.4
  555.7 2.3 copy-start.3
  558.1 2.3 copy-start.2
  560.4 2.3 copy-start.1
  564.3 250.9 %collective-permute-start.13 = (f32[256,2048]{1,0:T(8,128)}, f32[256,2048]{1,0:T(8,128)}, u32[]{:S(2)}, u32[]{:S(2)}) collective-permute-start(f32[256,2048]{1,0:T(8,128)} %bitcast.172), channel_id=1, source_target_pairs={{2,0},{3,1},{4,2},{5,3},{6,4},{7,5},{8,6},{9,7},{10,8},{11,9},{12,... | collective-permute-start | bytes 6291464 | tf_op jit(solution)/shard_map/ppermute | solution.py:18
  647.9 167.3 %collective-permute-start.14 = (f32[256,2048]{1,0:T(8,128)}, f32[256,2048]{1,0:T(8,128)}, u32[]{:S(2)}, u32[]{:S(2)}) collective-permute-start(f32[256,2048]{1,0:T(8,128)} %bitcast.171), channel_id=1, source_target_pairs={{3,0},{4,1},{5,2},{6,3},{7,4},{8,5},{9,6},{10,7},{11,8},{12,9},{13... | collective-permute-start | bytes 6291464 | tf_op jit(solution)/shard_map/ppermute | solution.py:18
  671.2 144.1 %collective-permute-start.15 = (f32[256,2048]{1,0:T(8,128)}, f32[256,2048]{1,0:T(8,128)}, u32[]{:S(2)}, u32[]{:S(2)}) collective-permute-start(f32[256,2048]{1,0:T(8,128)} %bitcast.170), channel_id=1, source_target_pairs={{4,0},{5,1},{6,2},{7,3},{8,4},{9,5},{10,6},{11,7},{12,8},{13,9},{1... | collective-permute-start | bytes 6291464 | tf_op jit(solution)/shard_map/ppermute | solution.py:18
  800.6 48.4 %collective-permute-start.16 = (f32[256,2048]{1,0:T(8,128)}, f32[256,2048]{1,0:T(8,128)}, u32[]{:S(2)}, u32[]{:S(2)}) collective-permute-start(f32[256,2048]{1,0:T(8,128)} %bitcast.169), channel_id=1, source_target_pairs={{5,0},{6,1},{7,2},{8,3},{9,4},{10,5},{11,6},{12,7},{13,8},{14,9},{... | collective-permute-start | bytes 6291464 | tf_op jit(solution)/shard_map/ppermute | solution.py:18
  802.6 271.1 %collective-permute-start.17 = (f32[256,2048]{1,0:T(8,128)}, f32[256,2048]{1,0:T(8,128)}, u32[]{:S(2)}, u32[]{:S(2)}) collective-permute-start(f32[256,2048]{1,0:T(8,128)} %bitcast.168), channel_id=1, source_target_pairs={{6,0},{7,1},{8,2},{9,3},{10,4},{11,5},{12,6},{13,7},{14,8},{15,9},... | collective-permute-start | bytes 6291464 | tf_op jit(solution)/shard_map/ppermute | solution.py:18
  808.3 265.4 %copy-start = (f32[16,32,8,128]{3,2,1,0:T(8,128)S(1)}, f32[16,32,8,128]{3,2,1,0:T(8,128)}, u32[]{:S(2)}) copy-start(f32[16,32,8,128]{3,2,1,0:T(8,128)} %get-tuple-element.295) | copy-start | bytes 6291460
  (3 other events, 2.9 us)
where the time goes:
time: 1090 us; the launch traced here: 1080 us
  waiting for transfers between devices  607 us (56%)
  matrix products  204 us (19%)
  starting transfers between devices  141 us (13%)
  local copies, waits for them, and re-layouts  106 us (10%)
  other arithmetic  21.2 us (2%)
    ppermute x24, waiting for transfers between devices, from_behind(): return lax.ppermute(block, axis, route)  607 us
    ppermute x24, starting transfers between devices, from_behind(): return lax.ppermute(block, axis, route)  141 us
    unnamed x76, local copies, waits for them, and re-layouts  79.4 us
    dot_general x32, matrix products, masked_scores(): jnp.einsum('td,kd->tk', query_head, key_head, preferred_element_type=jnp....  60.3 us
    dot_general x16, matrix products, backward_head(): jnp.einsum('tk,td->kd', score_low, query_head, preferred_element_type=jnp...  35.9 us
    dot_general x16, matrix products, backward_head(): jnp.dot(score_low, key_head, preferred_element_type=jnp.float32)  32.7 us
    dot_general x16, matrix products, forward_head(): jnp.dot(weights, value_head, preferred_element_type=jnp.float32)  30 us
    dot_general x16, matrix products, backward_head(): jnp.einsum('td,kd->tk', grad_head, value_head, preferred_element_type=jnp...  23.3 us
  transfers between devices with their start and end apart: 24, of which 17 were waited for; matrix products, arithmetic and copies ran while one was open for 6% of the time, Pallas kernels for 0%

commit v1 on v0

v1 whole, which is shorter than its diff:
```python
import functools
import math

import jax
import jax.numpy as jnp
from jax import lax
from jax.experimental import pallas as pl
from jax.experimental.pallas import tpu as pltpu
from jax.sharding import PartitionSpec as P

HEAD_DIM = 128
REACH = 6
RING = 8
HEADS_EACH = 2
NEG_FILL = -1e30
SCALE = 1.0 / math.sqrt(HEAD_DIM)
SCALE_LOG2 = SCALE * math.log2(math.e)
MESH = pl.DeviceIdType.MESH


def dot_nt(a, b):
    return lax.dot_general(a, b, (((1,), (1,)), ((), ())), preferred_element_type=jnp.float32)


def dot_nn(a, b):
    return jnp.dot(a, b, preferred_element_type=jnp.float32)


def kernel(
    n_blk, tok,
    doc_lengths, q_in, k_in, v_in, g_in,
    o_out, dq_out, dk_out, dv_out,
    k_buf, v_buf, q_buf, g_buf, kt, vt, start_ref,
    s_ref, d_ref, p_ref, ds_ref, acc_k, acc_v,
    o_stage, kv_stage, halo_send, halo_recv,
    in_send, in_recv, fwd_send, fwd_recv, back_send, back_recv, out_send, out_recv,
):
    me = lax.axis_index("blk")
    group, rank = me // RING, lax.rem(me, RING)
    n_groups = n_blk // RING
    window = (REACH + 1) * tok
    halo = REACH * tok

    def ring_device(member):
        return {"blk": group * RING + member}

    next_device = {"blk": lax.rem(group + 1, n_groups) * RING + rank}
    prev_device = {"blk": lax.rem(group + n_groups - 1, n_groups) * RING + rank}

    def member(k):
        return lax.rem(rank + k + RING, RING)

    def head_cols(owner, hh):
        return pl.ds(pl.multiple_of((owner * HEADS_EACH + hh) * HEAD_DIM, HEAD_DIM), HEAD_DIM)

    def rows(shard):
        return pl.ds(pl.multiple_of(shard * tok, tok), tok)

    def landed(ref, sem):
        pltpu.make_async_copy(ref, ref, sem).wait()

    sources = (k_in, v_in, q_in, g_in)

    def slot(hh, a, shard):
        if a < 2:
            return (k_buf, v_buf)[a].at[hh, rows(shard + REACH), :]
        return (q_buf, g_buf)[a - 2].at[hh, rows(shard), :]

    def in_copy(hh, a, target):
        return pltpu.make_async_remote_copy(
            src_ref=sources[a].at[:, head_cols(target, hh)],
            dst_ref=slot(hh, a, rank),
            send_sem=in_send.at[hh, a, target],
            recv_sem=in_recv.at[hh, a, rank],
            device_id=ring_device(target),
            device_id_type=MESH,
        )

    def own_copy(hh, a):
        return pltpu.make_async_copy(
            sources[a].at[:, head_cols(rank, hh)], slot(hh, a, rank), in_recv.at[hh, a, rank]
        )

    def in_landed(hh, a, shard):
        landed(slot(hh, a, shard), in_recv.at[hh, a, shard])

    def fwd_copy(hh, a, shard):
        h = shard - (RING - REACH)
        return pltpu.make_async_remote_copy(
            src_ref=slot(hh, a, shard),
            dst_ref=(k_buf, v_buf)[a].at[hh, rows(h), :],
            send_sem=fwd_send.at[hh, a, h],
            recv_sem=fwd_recv.at[hh, a, h],
            device_id=next_device,
            device_id_type=MESH,
        )

    def forward(hh, shard):
        for a in range(2):
            in_landed(hh, a, shard)

        @pl.when(shard >= RING - REACH)
        def _():
            for a in range(2):
                fwd_copy(hh, a, shard).start()

    def back_copy(hh, a, h):
        return pltpu.make_async_remote_copy(
            src_ref=halo_send.at[hh, a, rows(h), :],
            dst_ref=halo_recv.at[hh, a, rows(h), :],
            send_sem=back_send.at[hh, a, h],
            recv_sem=back_recv.at[hh, a, h],
            device_id=prev_device,
            device_id_type=MESH,
        )

    results = (o_out, dq_out, dk_out, dv_out)

    def staged(hh, a, shard):
        if a < 2:
            return o_stage.at[hh, a, rows(shard), :]
        return kv_stage.at[hh, a - 2, rows(shard), :]

    def out_copy(hh, a, target):
        return pltpu.make_async_remote_copy(
            src_ref=staged(hh, a, target),
            dst_ref=results[a].at[:, head_cols(rank, hh)],
            send_sem=out_send.at[hh, a, target],
            recv_sem=out_recv.at[hh, a, rank],
            device_id=ring_device(target),
            device_id_type=MESH,
        )

    def send_results(hh, first, target):
        @pl.when(target != rank)
        def _():
            for a in (first, first + 1):
                out_copy(hh, a, target).start()

        @pl.when(target == rank)
        def _():
            for a in (first, first + 1):
                pltpu.make_async_copy(
                    staged(hh, a, target),
                    results[a].at[:, head_cols(rank, hh)],
                    out_recv.at[hh, a, rank],
                ).start()

    barrier = pltpu.get_barrier_semaphore()
    for k in range(1, RING):
        pl.semaphore_signal(barrier, inc=1, device_id=ring_device(member(k)), device_id_type=MESH)
    pl.semaphore_signal(barrier, inc=1, device_id=next_device, device_id_type=MESH)
    pl.semaphore_signal(barrier, inc=1, device_id=prev_device, device_id_type=MESH)
    pl.semaphore_wait(barrier, RING + 1)

    def start_kv0(k, _):
        for a in (0, 1):
            in_copy(0, a, member(k)).start()
        return 0

    lax.fori_loop(1, RING, start_kv0, 0)
    for hh in range(HEADS_EACH):
        for a in range(4):
            own_copy(hh, a).start()

    position = group * RING * tok + (
        lax.broadcasted_iota(jnp.int32, (RING, tok), 0) * tok
        + lax.broadcasted_iota(jnp.int32, (RING, tok), 1)
    )
    first_key = jnp.zeros((RING, tok), jnp.int32)
    doc_end = jnp.int32(0)
    for j in range(doc_lengths.shape[0]):
        doc_end = doc_end + doc_lengths[j]
        first_key = jnp.where(position >= doc_end, doc_end, first_key)
    window_base = group * RING * tok - halo + lax.broadcasted_iota(jnp.int32, (RING, tok), 0) * tok
    start_ref[...] = first_key - window_base

    forward(0, rank)

    def start_qg0(k, _):
        target = member(k)
        for a in (0, 1):
            in_copy(0, a, target).wait_send()
        for a in (2, 3):
            in_copy(0, a, target).start()
        forward(0, member(-k))
        return 0

    lax.fori_loop(1, RING, start_qg0, 0)

    def start_kv1(k, _):
        target = member(k)
        for a in (2, 3):
            in_copy(0, a, target).wait_send()
        for a in (0, 1):
            in_copy(1, a, target).start()
        return 0

    lax.fori_loop(1, RING, start_kv1, 0)
    forward(1, rank)

    def transposed(hh, shard):
        kt[:, rows(shard)] = k_buf[hh, rows(shard), :].T
        vt[:, rows(shard)] = v_buf[hh, rows(shard), :].T

    key_row = lax.broadcasted_iota(jnp.int32, (tok, tok), 0)
    query_col = lax.broadcasted_iota(jnp.int32, (tok, tok), 1)

    def attend(hh, i):
        win = pl.ds(pl.multiple_of(i * tok, tok), window)
        q = q_buf[hh, rows(i), :]
        g = g_buf[hh, rows(i), :]
        start = start_ref[pl.ds(i, 1), :]
        s_ref[...] = dot_nt(k_buf[hh, win, :], q)
        top = None
        for b in range(REACH + 1):
            block = pl.ds(b * tok, tok)
            allowed = key_row >= start - b * tok
            if b == REACH:
                allowed = allowed & (key_row <= query_col)
            s = jnp.where(allowed, s_ref[block, :], NEG_FILL)
            s_ref[block, :] = s
            block_top = jnp.max(s, axis=0, keepdims=True)
            top = block_top if top is None else jnp.maximum(top, block_top)
        top = top * SCALE_LOG2
        total = None
        for b in range(REACH + 1):
            block = pl.ds(b * tok, tok)
            p = jnp.exp2(s_ref[block, :] * SCALE_LOG2 - top)
            s_ref[block, :] = p
            block_total = jnp.sum(p, axis=0, keepdims=True)
            total = block_total if total is None else total + block_total
        inverse = 1.0 / total
        for b in range(REACH + 1):
            block = pl.ds(b * tok, tok)
            p = s_ref[block, :] * inverse
            s_ref[block, :] = p
            p_ref[block, :] = p.astype(jnp.bfloat16)
        attended = dot_nn(vt[:, win], p_ref[...]).astype(jnp.bfloat16)
        o_stage[hh, 0, rows(i), :] = attended.T
        delta = jnp.sum(
            attended.astype(jnp.float32) * g.T.astype(jnp.float32), axis=0, keepdims=True
        )
        d_ref[...] = dot_nt(v_buf[hh, win, :], g)
        for b in range(REACH + 1):
            block = pl.ds(b * tok, tok)
            ds_ref[block, :] = (s_ref[block, :] * (d_ref[block, :] - delta)).astype(jnp.bfloat16)
        dq = dot_nn(kt[:, win], ds_ref[...]) * SCALE
        acc_k[win, :] += dot_nn(ds_ref[...], q)
        acc_v[win, :] += dot_nn(p_ref[...], g)
        o_stage[hh, 1, rows(i), :] = dq.astype(jnp.bfloat16).T

    def step(t, _):
        hh, i = t // RING, lax.rem(t, RING)

        @pl.when(i == 0)
        def _():
            acc_k[...] = jnp.zeros_like(acc_k)
            acc_v[...] = jnp.zeros_like(acc_v)

            def one(h, _):
                landed(k_buf.at[hh, rows(h), :], fwd_recv.at[hh, 0, h])
                landed(v_buf.at[hh, rows(h), :], fwd_recv.at[hh, 1, h])
                transposed(hh, h)
                return 0

            lax.fori_loop(0, REACH, one, 0)

        @pl.when((t >= 1) & (t < RING))
        def _():
            target = member(t)
            for a in (0, 1):
                in_copy(1, a, target).wait_send()
            for a in (2, 3):
                in_copy(1, a, target).start()
            forward(1, member(-t))

        for a in (2, 3):
            in_landed(hh, a, i)
        transposed(hh, i + REACH)
        attend(hh, i)
        send_results(hh, 0, i)

        @pl.when(i < REACH)
        def _():
            halo_send[hh, 0, rows(i), :] = (acc_k[rows(i), :] * SCALE).astype(jnp.bfloat16)
            halo_send[hh, 1, rows(i), :] = acc_v[rows(i), :].astype(jnp.bfloat16)
            for a in range(2):
                back_copy(hh, a, i).start()

        @pl.when(i == RING - 1)
        def _():
            def finish(shard, _):
                def put(dk, dv):
                    kv_stage[hh, 0, rows(shard), :] = dk.astype(jnp.bfloat16)
                    kv_stage[hh, 1, rows(shard), :] = dv.astype(jnp.bfloat16)

                own = rows(shard + REACH)

                @pl.when(shard < RING - REACH)
                def _():
                    put(acc_k[own, :] * SCALE, acc_v[own, :])

                @pl.when(shard >= RING - REACH)
                def _():
                    h = shard - (RING - REACH)
                    for a in range(2):
                        landed(halo_recv.at[hh, a, rows(h), :], back_recv.at[hh, a, h])
                    put(
                        acc_k[own, :] * SCALE + halo_recv[hh, 0, rows(h), :].astype(jnp.float32),
                        acc_v[own, :] + halo_recv[hh, 1, rows(h), :].astype(jnp.float32),
                    )

                send_results(hh, 2, shard)
                return 0

            lax.fori_loop(0, RING, finish, 0)

        return 0

    lax.fori_loop(0, HEADS_EACH * RING, step, 0)

    def drain(k, _):
        target = member(k)
        for a in (2, 3):
            in_copy(1, a, target).wait_send()
        for hh in range(HEADS_EACH):
            for a in range(4):
                out_copy(hh, a, target).wait_send()
        return 0

    lax.fori_loop(1, RING, drain, 0)

    def drain_halo(h, _):
        for hh in range(HEADS_EACH):
            for a in range(2):
                fwd_copy(hh, a, h + RING - REACH).wait_send()
                back_copy(hh, a, h).wait_send()
        return 0

    lax.fori_loop(0, REACH, drain_halo, 0)

    def drain_results(source, _):
        for hh in range(HEADS_EACH):
            for a in range(4):
                landed(results[a].at[:, head_cols(source, hh)], out_recv.at[hh, a, source])
        return 0

    lax.fori_loop(0, RING, drain_results, 0)


def solution(mesh):
    n_blk = mesh.shape["blk"]

    def on_device(queries, key_rows, value_rows, out_grad, doc_lengths):
        tok, width = queries.shape
        group_rows, keys = RING * tok, (RING + REACH) * tok
        halo, window = REACH * tok, (REACH + 1) * tok
        low, full = jnp.bfloat16, jnp.float32
        dma = pltpu.SemaphoreType.DMA
        out = jax.ShapeDtypeStruct((tok, width), low)
        any_space = pl.BlockSpec(memory_space=pl.ANY)
        flops = 6 * 2 * HEADS_EACH * RING * tok * window * HEAD_DIM
        return pl.pallas_call(
            functools.partial(kernel, n_blk, tok),
            out_shape=[out] * 4,
            in_specs=[pl.BlockSpec(memory_space=pltpu.SMEM)] + [any_space] * 4,
            out_specs=[any_space] * 4,
            scratch_shapes=[
                pltpu.VMEM((HEADS_EACH, keys, HEAD_DIM), low),
                pltpu.VMEM((HEADS_EACH, keys, HEAD_DIM), low),
                pltpu.VMEM((HEADS_EACH, group_rows, HEAD_DIM), low),
                pltpu.VMEM((HEADS_EACH, group_rows, HEAD_DIM), low),
                pltpu.VMEM((HEAD_DIM, keys), low),
                pltpu.VMEM((HEAD_DIM, keys), low),
                pltpu.VMEM((RING, tok), jnp.int32),
                pltpu.VMEM((window, tok), full),
                pltpu.VMEM((window, tok), full),
                pltpu.VMEM((window, tok), low),
                pltpu.VMEM((window, tok), low),
                pltpu.VMEM((keys, HEAD_DIM), full),
                pltpu.VMEM((keys, HEAD_DIM), full),
                pltpu.VMEM((HEADS_EACH, 2, group_rows, HEAD_DIM), low),
                pltpu.VMEM((HEADS_EACH, 2, group_rows, HEAD_DIM), low),
                pltpu.VMEM((HEADS_EACH, 2, halo, HEAD_DIM), low),
                pltpu.VMEM((HEADS_EACH, 2, halo, HEAD_DIM), low),
                dma((HEADS_EACH, 4, RING)),
                dma((HEADS_EACH, 4, RING)),
                dma((HEADS_EACH, 2, REACH)),
                dma((HEADS_EACH, 2, REACH)),
                dma((HEADS_EACH, 2, REACH)),
                dma((HEADS_EACH, 2, REACH)),
                dma((HEADS_EACH, 4, RING)),
                dma((HEADS_EACH, 4, RING)),
            ],
            compiler_params=pltpu.CompilerParams(
                collective_id=0, has_side_effects=True, vmem_limit_bytes=56 * 2**20
            ),
            cost_estimate=pl.CostEstimate(
                flops=flops, bytes_accessed=16 * tok * width, transcendentals=0
            ),
        )(doc_lengths, queries, key_rows, value_rows, out_grad)

    rows_spec = P(("dp", "blk"), None)
    return jax.shard_map(
        on_device,
        mesh=mesh,
        in_specs=(rows_spec,) * 4 + (P("dp"),),
        out_specs=(rows_spec,) * 4,
        check_vma=False,
    )
```

time: 1090 us -> 114 us (0.10)
  the two profiles are of different devices: /device:TPU:56 before, /device:TPU:1 now
where the time goes in v1:
time: 114 us
  Pallas kernels  106 us (93%)
  local copies, waits for them, and re-layouts  6.57 us (6%)
    pallas_call x1, Pallas kernels, on_device(): pl.pallas_call(functools.partial(kernel, n_blk, tok), out_shape=[out] * 4...  106 us
    unnamed x10, local copies, waits for them, and re-layouts  6.57 us

profile of v1, /device:TPU:1, one launch (start us, length us, event | category | flops | bytes accessed | tf_op | source)
XLA Modules:
  0.0 113.5 jit_solution(11795314255412441468)
XLA Ops:
  0.6 106.3 %shard_map.84 = (bf16[256,2048]{1,0:T(8,128)(2,1)}, bf16[256,2048]{1,0:T(8,128)(2,1)}, bf16[256,2048]{1,0:T(8,128)(2,1)}, bf16[256,2048]{1,0:T(8,128)(2,1)}) custom-call(s32[16]{0:T(128)} %doc_lengths.1, bf16[256,2048]{1,0:T(8,128)(2,1)} %q_in.1, bf16[256,2048]{1,0:T(8,128)(2,1)} %k_in.1, bf16[256,2048]{1,0:T(8,128)(2,1)} %v_in.1, bf16[256,2048]{1,0:T(8,128)(2,1)} %g_in.1), custom_call_target="tpu_custom_call" | custom-call | flops 11274289152 | bytes 8388608 | tf_op jit(solution)/shard_map/pallas_call | solution.py:364
  106.9 0.0 copy-start.2
  106.9 2.4 %copy.13 = bf16[256,2048]{1,0:T(8,128)(2,1)} copy(bf16[256,2048]{1,0:T(8,128)(2,1)} %get-tuple-element.8) | data formatting | bytes 2097152
  109.3 0.0 copy-done.2
  109.3 0.0 copy-start.1
  109.3 1.0 copy.14
  110.3 0.6 copy-done.1
  110.9 0.0 copy-start
  110.9 1.0 copy.15
  111.9 0.6 copy-done
  112.5 1.0 copy.16
Async XLA Ops:
  106.9 2.4 %copy-start.2 = (bf16[256,2048]{1,0:T(8,128)(2,1)S(1)}, bf16[256,2048]{1,0:T(8,128)(2,1)}, u32[]{:S(2)}) copy-start(bf16[256,2048]{1,0:T(8,128)(2,1)} %get-tuple-element.9) | copy-start | bytes 3145732
  109.3 1.6 %copy-start.1 = (bf16[256,2048]{1,0:T(8,128)(2,1)S(1)}, bf16[256,2048]{1,0:T(8,128)(2,1)}, u32[]{:S(2)}) copy-start(bf16[256,2048]{1,0:T(8,128)(2,1)} %get-tuple-element.10) | copy-start | bytes 3145732
  110.9 1.6 %copy-start = (bf16[256,2048]{1,0:T(8,128)(2,1)S(1)}, bf16[256,2048]{1,0:T(8,128)(2,1)}, u32[]{:S(2)}) copy-start(bf16[256,2048]{1,0:T(8,128)(2,1)} %get-tuple-element.11) | copy-start | bytes 3145732

commit v2 on v1

--- a/solution.py
+++ b/solution.py
@@ -12,6 +12,7 @@
 REACH = 6
 RING = 8
 HEADS_EACH = 2
+PIECES = 2
 NEG_FILL = -1e30
 SCALE = 1.0 / math.sqrt(HEAD_DIM)
 SCALE_LOG2 = SCALE * math.log2(math.e)
@@ -290,7 +291,9 @@
 
         @pl.when(i == RING - 1)
         def _():
-            def finish(shard, _):
+            def finish(k, _):
+                shard = member(k)
+
                 def put(dk, dv):
                     kv_stage[hh, 0, rows(shard), :] = dk.astype(jnp.bfloat16)
                     kv_stage[hh, 1, rows(shard), :] = dv.astype(jnp.bfloat16)
@@ -349,6 +352,24 @@
     lax.fori_loop(0, RING, drain_results, 0)
 
 
+def write_out(*refs):
+    sources, targets, sems = refs[:4], refs[4:8], refs[8]
+    part = sources[0].shape[0] // PIECES
+    copies = [
+        pltpu.make_async_copy(
+            sources[a].at[pl.ds(n * part, part), :],
+            targets[a].at[pl.ds(n * part, part), :],
+            sems.at[a, n],
+        )
+        for n in range(PIECES)
+        for a in range(4)
+    ]
+    for copy in copies:
+        copy.start()
+    for copy in copies:
+        copy.wait()
+
+
 def solution(mesh):
     n_blk = mesh.shape["blk"]
 
@@ -358,12 +379,13 @@
         halo, window = REACH * tok, (REACH + 1) * tok
         low, full = jnp.bfloat16, jnp.float32
         dma = pltpu.SemaphoreType.DMA
+        landing = pltpu.VMEM((tok, width), low)
         out = jax.ShapeDtypeStruct((tok, width), low)
         any_space = pl.BlockSpec(memory_space=pl.ANY)
         flops = 6 * 2 * HEADS_EACH * RING * tok * window * HEAD_DIM
-        return pl.pallas_call(
+        results = pl.pallas_call(
             functools.partial(kernel, n_blk, tok),
-            out_shape=[out] * 4,
+            out_shape=[landing] * 4,
             in_specs=[pl.BlockSpec(memory_space=pltpu.SMEM)] + [any_space] * 4,
             out_specs=[any_space] * 4,
             scratch_shapes=[
@@ -394,12 +416,23 @@
                 dma((HEADS_EACH, 4, RING)),
             ],
             compiler_params=pltpu.CompilerParams(
-                collective_id=0, has_side_effects=True, vmem_limit_bytes=56 * 2**20
+                collective_id=0, has_side_effects=True, vmem_limit_bytes=58 * 2**20
             ),
             cost_estimate=pl.CostEstimate(
                 flops=flops, bytes_accessed=16 * tok * width, transcendentals=0
             ),
         )(doc_lengths, queries, key_rows, value_rows, out_grad)
+        return pl.pallas_call(
+            write_out,
+            out_shape=[out] * 4,
+            in_specs=[any_space] * 4,
+            out_specs=[any_space] * 4,
+            scratch_shapes=[dma((4, PIECES))],
+            compiler_params=pltpu.CompilerParams(vmem_limit_bytes=2**20),
+            cost_estimate=pl.CostEstimate(
+                flops=0, bytes_accessed=16 * tok * width, transcendentals=0
+            ),
+        )(*[pltpu.with_memory_space_constraint(r, pltpu.VMEM) for r in results])
 
     rows_spec = P(("dp", "blk"), None)
     return jax.shard_map(

time: 114 us -> 109 us (0.956)
  local copies, waits for them, and re-layouts: 6.57 us -> 0 us
  Pallas kernels: 106 us -> 108 us
    unnamed x10 -> x0, local copies, waits for them, and re-layouts: 6.57 us -> none
    pallas_call x1 -> x2, Pallas kernels: 106 us -> 108 us  [the longest x1 106 us: on_device(): pl.pallas_call(functools.partial(kernel, n_blk, tok), out_shape=[landing]...]
where the time goes in v2:
time: 109 us
  Pallas kernels  108 us (99%)
    pallas_call x1, Pallas kernels, on_device(): pl.pallas_call(functools.partial(kernel, n_blk, tok), out_shape=[landing]...  106 us

profile of v2, /device:TPU:1, one launch (start us, length us, event | category | flops | bytes accessed | tf_op | source)
XLA Modules:
  0.0 109.0 jit_solution(15986869051044665623)
XLA Ops:
  0.6 106.3 %shard_map.84 = (bf16[256,2048]{1,0:T(8,128)(2,1)S(1)}, bf16[256,2048]{1,0:T(8,128)(2,1)S(1)}, bf16[256,2048]{1,0:T(8,128)(2,1)S(1)}, bf16[256,2048]{1,0:T(8,128)(2,1)S(1)}) custom-call(s32[16]{0:T(128)} %doc_lengths.1, bf16[256,2048]{1,0:T(8,128)(2,1)} %q_in.1, bf16[256,2048]{1,0:T(8,128)(2,1)} %k_in.1, bf16[256,2048]{1,0:T(8,128)(2,1)} %v_in.1, ...), custom_call_target="tpu_custom_call" | custom-call | flops 11274289152 | bytes 8388608 | tf_op jit(solution)/shard_map/pallas_call | solution.py:386
  106.9 2.1 %shard_map.85 = (bf16[256,2048]{1,0:T(8,128)(2,1)}, bf16[256,2048]{1,0:T(8,128)(2,1)}, bf16[256,2048]{1,0:T(8,128)(2,1)}, bf16[256,2048]{1,0:T(8,128)(2,1)}) custom-call(bf16[256,2048]{1,0:T(8,128)(2,1)S(1)} %get-tuple-element.8.refs_0_, bf16[256,2048]{1,0:T(8,128)(2,1)S(1)} %get-tuple-element.9.refs_1_, bf16[256,2048]{1,0:T(8,128)(2,1)S(1)} %get-tuple-element.10.refs_2_, ...), custom_call_target="tpu_custom_call" | custom-call | bytes 8388608 | tf_op jit(solution)/shard_map/pallas_call | solution.py:425

commit v3 on v2

--- a/solution.py
+++ b/solution.py
@@ -12,7 +12,8 @@
 REACH = 6
 RING = 8
 HEADS_EACH = 2
-PIECES = 2
+PIECES = 1
+WINDOW = 12
 NEG_FILL = -1e30
 SCALE = 1.0 / math.sqrt(HEAD_DIM)
 SCALE_LOG2 = SCALE * math.log2(math.e)
@@ -45,6 +46,7 @@
     def ring_device(member):
         return {"blk": group * RING + member}
 
+    has_prev, has_next = group > 0, group < n_groups - 1
     next_device = {"blk": lax.rem(group + 1, n_groups) * RING + rank}
     prev_device = {"blk": lax.rem(group + n_groups - 1, n_groups) * RING + rank}
 
@@ -100,7 +102,7 @@
         for a in range(2):
             in_landed(hh, a, shard)
 
-        @pl.when(shard >= RING - REACH)
+        @pl.when((shard >= RING - REACH) & has_next)
         def _():
             for a in range(2):
                 fwd_copy(hh, a, shard).start()
@@ -126,8 +128,8 @@
         return pltpu.make_async_remote_copy(
             src_ref=staged(hh, a, target),
             dst_ref=results[a].at[:, head_cols(rank, hh)],
-            send_sem=out_send.at[hh, a, target],
-            recv_sem=out_recv.at[hh, a, rank],
+            send_sem=out_send.at[a],
+            recv_sem=out_recv.at[a],
             device_id=ring_device(target),
             device_id_type=MESH,
         )
@@ -144,25 +146,50 @@
                 pltpu.make_async_copy(
                     staged(hh, a, target),
                     results[a].at[:, head_cols(rank, hh)],
-                    out_recv.at[hh, a, rank],
+                    out_recv.at[a],
                 ).start()
 
     barrier = pltpu.get_barrier_semaphore()
     for k in range(1, RING):
         pl.semaphore_signal(barrier, inc=1, device_id=ring_device(member(k)), device_id_type=MESH)
-    pl.semaphore_signal(barrier, inc=1, device_id=next_device, device_id_type=MESH)
-    pl.semaphore_signal(barrier, inc=1, device_id=prev_device, device_id_type=MESH)
-    pl.semaphore_wait(barrier, RING + 1)
-
-    def start_kv0(k, _):
-        for a in (0, 1):
-            in_copy(0, a, member(k)).start()
-        return 0
-
-    lax.fori_loop(1, RING, start_kv0, 0)
+
+    @pl.when(has_next)
+    def _():
+        pl.semaphore_signal(barrier, inc=1, device_id=next_device, device_id_type=MESH)
+
+    @pl.when(has_prev)
+    def _():
+        pl.semaphore_signal(barrier, inc=1, device_id=prev_device, device_id_type=MESH)
+
+    pl.semaphore_wait(barrier, RING - 1 + has_next.astype(jnp.int32) + has_prev.astype(jnp.int32))
+
+    sends = [(hh, a, k) for hh in range(HEADS_EACH) for a in (0, 2) for k in range(1, RING)]
+    paced = (2 * HEADS_EACH - 1) * (RING - 1)
+
+    def start_send(n):
+        hh, a, k = sends[n]
+        for b in (a, a + 1):
+            in_copy(hh, b, member(k)).start()
+
+    def wait_send(n):
+        hh, a, k = sends[n]
+        for b in (a, a + 1):
+            in_copy(hh, b, member(k)).wait_send()
+
+    for n in range(WINDOW):
+        start_send(n)
     for hh in range(HEADS_EACH):
         for a in range(4):
             own_copy(hh, a).start()
+
+    @pl.when(jnp.logical_not(has_prev))
+    def _():
+        for buf in (k_buf, v_buf):
+            buf[:, :halo, :] = jnp.zeros((HEADS_EACH, halo, HEAD_DIM), buf.dtype)
+
+    @pl.when(jnp.logical_not(has_next))
+    def _():
+        halo_recv[...] = jnp.zeros_like(halo_recv)
 
     position = group * RING * tok + (
         lax.broadcasted_iota(jnp.int32, (RING, tok), 0) * tok
@@ -178,26 +205,11 @@
 
     forward(0, rank)
 
-    def start_qg0(k, _):
-        target = member(k)
-        for a in (0, 1):
-            in_copy(0, a, target).wait_send()
-        for a in (2, 3):
-            in_copy(0, a, target).start()
-        forward(0, member(-k))
-        return 0
-
-    lax.fori_loop(1, RING, start_qg0, 0)
-
-    def start_kv1(k, _):
-        target = member(k)
-        for a in (2, 3):
-            in_copy(0, a, target).wait_send()
-        for a in (0, 1):
-            in_copy(1, a, target).start()
-        return 0
-
-    lax.fori_loop(1, RING, start_kv1, 0)
+    for n in range(WINDOW, paced):
+        wait_send(n - WINDOW)
+        start_send(n)
+        if n - WINDOW < RING - 1:
+            forward(0, member(-(n - WINDOW + 1)))
     forward(1, rank)
 
     def transposed(hh, shard):
@@ -260,20 +272,28 @@
             acc_v[...] = jnp.zeros_like(acc_v)
 
             def one(h, _):
-                landed(k_buf.at[hh, rows(h), :], fwd_recv.at[hh, 0, h])
-                landed(v_buf.at[hh, rows(h), :], fwd_recv.at[hh, 1, h])
+                @pl.when(has_prev)
+                def _():
+                    landed(k_buf.at[hh, rows(h), :], fwd_recv.at[hh, 0, h])
+                    landed(v_buf.at[hh, rows(h), :], fwd_recv.at[hh, 1, h])
+
                 transposed(hh, h)
                 return 0
 
             lax.fori_loop(0, REACH, one, 0)
 
+        @pl.when(t * 2 < RING - 1)
+        def _():
+            for n in range(2):
+                k = t * 2 + n + 1
+
+                @pl.when(k < RING)
+                def _():
+                    for a in (2, 3):
+                        in_copy(1, a, member(k)).start()
+
         @pl.when((t >= 1) & (t < RING))
         def _():
-            target = member(t)
-            for a in (0, 1):
-                in_copy(1, a, target).wait_send()
-            for a in (2, 3):
-                in_copy(1, a, target).start()
             forward(1, member(-t))
 
         for a in (2, 3):
@@ -282,7 +302,7 @@
         attend(hh, i)
         send_results(hh, 0, i)
 
-        @pl.when(i < REACH)
+        @pl.when((i < REACH) & has_prev)
         def _():
             halo_send[hh, 0, rows(i), :] = (acc_k[rows(i), :] * SCALE).astype(jnp.bfloat16)
             halo_send[hh, 1, rows(i), :] = acc_v[rows(i), :].astype(jnp.bfloat16)
@@ -307,8 +327,12 @@
                 @pl.when(shard >= RING - REACH)
                 def _():
                     h = shard - (RING - REACH)
-                    for a in range(2):
-                        landed(halo_recv.at[hh, a, rows(h), :], back_recv.at[hh, a, h])
+
+                    @pl.when(has_next)
+                    def _():
+                        for a in range(2):
+                            landed(halo_recv.at[hh, a, rows(h), :], back_recv.at[hh, a, h])
+
                     put(
                         acc_k[own, :] * SCALE + halo_recv[hh, 0, rows(h), :].astype(jnp.float32),
                         acc_v[own, :] + halo_recv[hh, 1, rows(h), :].astype(jnp.float32),
@@ -323,33 +347,26 @@
 
     lax.fori_loop(0, HEADS_EACH * RING, step, 0)
 
-    def drain(k, _):
-        target = member(k)
-        for a in (2, 3):
-            in_copy(1, a, target).wait_send()
-        for hh in range(HEADS_EACH):
-            for a in range(4):
-                out_copy(hh, a, target).wait_send()
-        return 0
-
-    lax.fori_loop(1, RING, drain, 0)
-
+    for n in range(paced - WINDOW, len(sends)):
+        wait_send(n)
     def drain_halo(h, _):
         for hh in range(HEADS_EACH):
             for a in range(2):
-                fwd_copy(hh, a, h + RING - REACH).wait_send()
-                back_copy(hh, a, h).wait_send()
+                @pl.when(has_next)
+                def _():
+                    fwd_copy(hh, a, h + RING - REACH).wait_send()
+
+                @pl.when(has_prev)
+                def _():
+                    back_copy(hh, a, h).wait_send()
+
         return 0
 
     lax.fori_loop(0, REACH, drain_halo, 0)
 
-    def drain_results(source, _):
-        for hh in range(HEADS_EACH):
-            for a in range(4):
-                landed(results[a].at[:, head_cols(source, hh)], out_recv.at[hh, a, source])
-        return 0
-
-    lax.fori_loop(0, RING, drain_results, 0)
+    for a in range(4):
+        landed(k_buf.at[0], out_send.at[a])
+        landed(results[a], out_recv.at[a])
 
 
 def write_out(*refs):
@@ -412,8 +429,8 @@
                 dma((HEADS_EACH, 2, REACH)),
                 dma((HEADS_EACH, 2, REACH)),
                 dma((HEADS_EACH, 2, REACH)),
-                dma((HEADS_EACH, 4, RING)),
-                dma((HEADS_EACH, 4, RING)),
+                dma((4,)),
+                dma((4,)),
             ],
             compiler_params=pltpu.CompilerParams(
                 collective_id=0, has_side_effects=True, vmem_limit_bytes=58 * 2**20

time: 109 us -> 104 us (0.954)
  Pallas kernels: 108 us -> 103 us
    pallas_call x1, Pallas kernels: 106 us -> 100 us  [on_device(): pl.pallas_call(functools.partial(kernel, n_blk, tok), out_shape=[landing]...]
where the time goes in v3:
time: 104 us; the launch traced here: 103 us
  Pallas kernels  103 us (99%)
    pallas_call x1, Pallas kernels, on_device(): pl.pallas_call(functools.partial(kernel, n_blk, tok), out_shape=[landing]...  100 us

profile of v3, /device:TPU:1, one launch (start us, length us, event | category | flops | bytes accessed | tf_op | source)
XLA Modules:
  0.0 103.2 jit_solution(2067825048342589105)
XLA Ops:
  0.6 100.5 %shard_map.84 = (bf16[256,2048]{1,0:T(8,128)(2,1)S(1)}, bf16[256,2048]{1,0:T(8,128)(2,1)S(1)}, bf16[256,2048]{1,0:T(8,128)(2,1)S(1)}, bf16[256,2048]{1,0:T(8,128)(2,1)S(1)}) custom-call(s32[16]{0:T(128)} %doc_lengths.1, bf16[256,2048]{1,0:T(8,128)(2,1)} %q_in.1, bf16[256,2048]{1,0:T(8,128)(2,1)} %k_in.1, bf16[256,2048]{1,0:T(8,128)(2,1)} %v_in.1, ...), custom_call_target="tpu_custom_call" | custom-call | flops 11274289152 | bytes 8388608 | tf_op jit(solution)/shard_map/pallas_call | solution.py:403
  101.1 2.0 %shard_map.85 = (bf16[256,2048]{1,0:T(8,128)(2,1)}, bf16[256,2048]{1,0:T(8,128)(2,1)}, bf16[256,2048]{1,0:T(8,128)(2,1)}, bf16[256,2048]{1,0:T(8,128)(2,1)}) custom-call(bf16[256,2048]{1,0:T(8,128)(2,1)S(1)} %get-tuple-element.8.refs_0_, bf16[256,2048]{1,0:T(8,128)(2,1)S(1)} %get-tuple-element.9.refs_1_, bf16[256,2048]{1,0:T(8,128)(2,1)S(1)} %get-tuple-element.10.refs_2_, ...), custom_call_target="tpu_custom_call" | custom-call | bytes 8388608 | tf_op jit(solution)/shard_map/pallas_call | solution.py:442

commit v4 on v3

--- a/solution.py
+++ b/solution.py
@@ -12,7 +12,6 @@
 REACH = 6
 RING = 8
 HEADS_EACH = 2
-PIECES = 1
 WINDOW = 12
 NEG_FILL = -1e30
 SCALE = 1.0 / math.sqrt(HEAD_DIM)
@@ -30,12 +29,13 @@
 
 def kernel(
     n_blk, tok,
-    doc_lengths, q_in, k_in, v_in, g_in,
-    o_out, dq_out, dk_out, dv_out,
+    doc_lengths_in, q_in, k_in, v_in, g_in,
+    results,
     k_buf, v_buf, q_buf, g_buf, kt, vt, start_ref,
     s_ref, d_ref, p_ref, ds_ref, acc_k, acc_v,
-    o_stage, kv_stage, halo_send, halo_recv,
+    stage, halo_send, halo_recv,
     in_send, in_recv, fwd_send, fwd_recv, back_send, back_recv, out_send, out_recv,
+    doc_lengths, doc_sem,
 ):
     me = lax.axis_index("blk")
     group, rank = me // RING, lax.rem(me, RING)
@@ -117,37 +117,27 @@
             device_id_type=MESH,
         )
 
-    results = (o_out, dq_out, dk_out, dv_out)
-
-    def staged(hh, a, shard):
-        if a < 2:
-            return o_stage.at[hh, a, rows(shard), :]
-        return kv_stage.at[hh, a - 2, rows(shard), :]
-
-    def out_copy(hh, a, target):
-        return pltpu.make_async_remote_copy(
-            src_ref=staged(hh, a, target),
-            dst_ref=results[a].at[:, head_cols(rank, hh)],
-            send_sem=out_send.at[a],
-            recv_sem=out_recv.at[a],
-            device_id=ring_device(target),
-            device_id_type=MESH,
-        )
+    def out_pair(hh, first, target):
+        pair = pl.ds(first, 2)
+        return stage.at[hh, pair, rows(target), :], results.at[pair, :, head_cols(rank, hh)]
 
     def send_results(hh, first, target):
+        source, landing = out_pair(hh, first, target)
+
         @pl.when(target != rank)
         def _():
-            for a in (first, first + 1):
-                out_copy(hh, a, target).start()
+            pltpu.make_async_remote_copy(
+                src_ref=source,
+                dst_ref=landing,
+                send_sem=out_send.at[first // 2],
+                recv_sem=out_recv.at[first // 2],
+                device_id=ring_device(target),
+                device_id_type=MESH,
+            ).start()
 
         @pl.when(target == rank)
         def _():
-            for a in (first, first + 1):
-                pltpu.make_async_copy(
-                    staged(hh, a, target),
-                    results[a].at[:, head_cols(rank, hh)],
-                    out_recv.at[a],
-                ).start()
+            pltpu.make_async_copy(source, landing, out_recv.at[first // 2]).start()
 
     barrier = pltpu.get_barrier_semaphore()
     for k in range(1, RING):
@@ -161,6 +151,8 @@
     def _():
         pl.semaphore_signal(barrier, inc=1, device_id=prev_device, device_id_type=MESH)
 
+    doc_copy = pltpu.make_async_copy(doc_lengths_in, doc_lengths, doc_sem)
+    doc_copy.start()
     pl.semaphore_wait(barrier, RING - 1 + has_next.astype(jnp.int32) + has_prev.astype(jnp.int32))
 
     sends = [(hh, a, k) for hh in range(HEADS_EACH) for a in (0, 2) for k in range(1, RING)]
@@ -195,6 +187,7 @@
         lax.broadcasted_iota(jnp.int32, (RING, tok), 0) * tok
         + lax.broadcasted_iota(jnp.int32, (RING, tok), 1)
     )
+    doc_copy.wait()
     first_key = jnp.zeros((RING, tok), jnp.int32)
     doc_end = jnp.int32(0)
     for j in range(doc_lengths.shape[0]):
@@ -250,7 +243,7 @@
             s_ref[block, :] = p
             p_ref[block, :] = p.astype(jnp.bfloat16)
         attended = dot_nn(vt[:, win], p_ref[...]).astype(jnp.bfloat16)
-        o_stage[hh, 0, rows(i), :] = attended.T
+        stage[hh, 0, rows(i), :] = attended.T
         delta = jnp.sum(
             attended.astype(jnp.float32) * g.T.astype(jnp.float32), axis=0, keepdims=True
         )
@@ -261,7 +254,7 @@
         dq = dot_nn(kt[:, win], ds_ref[...]) * SCALE
         acc_k[win, :] += dot_nn(ds_ref[...], q)
         acc_v[win, :] += dot_nn(p_ref[...], g)
-        o_stage[hh, 1, rows(i), :] = dq.astype(jnp.bfloat16).T
+        stage[hh, 1, rows(i), :] = dq.astype(jnp.bfloat16).T
 
     def step(t, _):
         hh, i = t // RING, lax.rem(t, RING)
@@ -315,8 +308,8 @@
                 shard = member(k)
 
                 def put(dk, dv):
-                    kv_stage[hh, 0, rows(shard), :] = dk.astype(jnp.bfloat16)
-                    kv_stage[hh, 1, rows(shard), :] = dv.astype(jnp.bfloat16)
+                    stage[hh, 2, rows(shard), :] = dk.astype(jnp.bfloat16)
+                    stage[hh, 3, rows(shard), :] = dv.astype(jnp.bfloat16)
 
                 own = rows(shard + REACH)
 
@@ -364,22 +357,15 @@
 
     lax.fori_loop(0, REACH, drain_halo, 0)
 
-    for a in range(4):
-        landed(k_buf.at[0], out_send.at[a])
-        landed(results[a], out_recv.at[a])
-
-
-def write_out(*refs):
-    sources, targets, sems = refs[:4], refs[4:8], refs[8]
-    part = sources[0].shape[0] // PIECES
+    for n in range(2):
+        landed(k_buf, out_send.at[n])
+        landed(results.at[pl.ds(2 * n, 2)], out_recv.at[n])
+
+
+def write_out(landing, *refs):
+    targets, sems = refs[:4], refs[4]
     copies = [
-        pltpu.make_async_copy(
-            sources[a].at[pl.ds(n * part, part), :],
-            targets[a].at[pl.ds(n * part, part), :],
-            sems.at[a, n],
-        )
-        for n in range(PIECES)
-        for a in range(4)
+        pltpu.make_async_copy(landing.at[a], targets[a], sems.at[a]) for a in range(4)
     ]
     for copy in copies:
         copy.start()
@@ -396,15 +382,15 @@
         halo, window = REACH * tok, (REACH + 1) * tok
         low, full = jnp.bfloat16, jnp.float32
         dma = pltpu.SemaphoreType.DMA
-        landing = pltpu.VMEM((tok, width), low)
+        landing = pltpu.VMEM((4, tok, width), low)
         out = jax.ShapeDtypeStruct((tok, width), low)
         any_space = pl.BlockSpec(memory_space=pl.ANY)
         flops = 6 * 2 * HEADS_EACH * RING * tok * window * HEAD_DIM
         results = pl.pallas_call(
             functools.partial(kernel, n_blk, tok),
-            out_shape=[landing] * 4,
-            in_specs=[pl.BlockSpec(memory_space=pltpu.SMEM)] + [any_space] * 4,
-            out_specs=[any_space] * 4,
+            out_shape=landing,
+            in_specs=[any_space] * 5,
+            out_specs=any_space,
             scratch_shapes=[
                 pltpu.VMEM((HEADS_EACH, keys, HEAD_DIM), low),
                 pltpu.VMEM((HEADS_EACH, keys, HEAD_DIM), low),
@@ -419,8 +405,7 @@
                 pltpu.VMEM((window, tok), low),
                 pltpu.VMEM((keys, HEAD_DIM), full),
                 pltpu.VMEM((keys, HEAD_DIM), full),
-                pltpu.VMEM((HEADS_EACH, 2, group_rows, HEAD_DIM), low),
-                pltpu.VMEM((HEADS_EACH, 2, group_rows, HEAD_DIM), low),
+                pltpu.VMEM((HEADS_EACH, 4, group_rows, HEAD_DIM), low),
                 pltpu.VMEM((HEADS_EACH, 2, halo, HEAD_DIM), low),
                 pltpu.VMEM((HEADS_EACH, 2, halo, HEAD_DIM), low),
                 dma((HEADS_EACH, 4, RING)),
@@ -429,8 +414,10 @@
                 dma((HEADS_EACH, 2, REACH)),
                 dma((HEADS_EACH, 2, REACH)),
                 dma((HEADS_EACH, 2, REACH)),
-                dma((4,)),
-                dma((4,)),
+                dma((2,)),
+                dma((2,)),
+                pltpu.SMEM(doc_lengths.shape, jnp.int32),
+                dma(()),
             ],
             compiler_params=pltpu.CompilerParams(
                 collective_id=0, has_side_effects=True, vmem_limit_bytes=58 * 2**20
@@ -442,14 +429,14 @@
         return pl.pallas_call(
             write_out,
             out_shape=[out] * 4,
-            in_specs=[any_space] * 4,
+            in_specs=[any_space],
             out_specs=[any_space] * 4,
-            scratch_shapes=[dma((4, PIECES))],
+            scratch_shapes=[dma((4,))],
             compiler_params=pltpu.CompilerParams(vmem_limit_bytes=2**20),
             cost_estimate=pl.CostEstimate(
                 flops=0, bytes_accessed=16 * tok * width, transcendentals=0
             ),
-        )(*[pltpu.with_memory_space_constraint(r, pltpu.VMEM) for r in results])
+        )(pltpu.with_memory_space_constraint(results, pltpu.VMEM))
 
     rows_spec = P(("dp", "blk"), None)
     return jax.shard_map(

time: 104 us -> 103 us (level)
  no operation moved by 1% of the time
where the time goes in v4:
time: 103 us; the launch traced here: 102 us
  Pallas kernels  102 us (99%)
    pallas_call x1, Pallas kernels, on_device(): pl.pallas_call(functools.partial(kernel, n_blk, tok), out_shape=landing,...  99.8 us

profile of v4, /device:TPU:1, one launch (start us, length us, event | category | flops | bytes accessed | tf_op | source)
XLA Modules:
  0.0 102.5 jit_solution(1332112553161241135)
XLA Ops:
  0.6 99.8 %shard_map.84.landing = bf16[4,256,2048]{2,1,0:T(8,128)(2,1)S(1)} custom-call(s32[16]{0:T(128)} %doc_lengths_in.1, bf16[256,2048]{1,0:T(8,128)(2,1)} %q_in.1, bf16[256,2048]{1,0:T(8,128)(2,1)} %k_in.1, bf16[256,2048]{1,0:T(8,128)(2,1)} %v_in.1, bf16[256,2048]{1,0:T(8,128)(2,1)} %g_in.1), custom_call_target="tpu_custom_call" | custom-call | flops 11274289152 | bytes 8388608 | tf_op jit(solution)/shard_map/pallas_call | solution.py:389
  100.4 2.0 %shard_map.85 = (bf16[256,2048]{1,0:T(8,128)(2,1)}, bf16[256,2048]{1,0:T(8,128)(2,1)}, bf16[256,2048]{1,0:T(8,128)(2,1)}, bf16[256,2048]{1,0:T(8,128)(2,1)}) custom-call(bf16[4,256,2048]{2,1,0:T(8,128)(2,1)S(1)} %shard_map.84.landing), custom_call_target="tpu_custom_call" | custom-call | bytes 8388608 | tf_op jit(solution)/shard_map/pallas_call | solution.py:429

commit v5 on v4

--- a/solution.py
+++ b/solution.py
@@ -35,7 +35,7 @@
     s_ref, d_ref, p_ref, ds_ref, acc_k, acc_v,
     stage, halo_send, halo_recv,
     in_send, in_recv, fwd_send, fwd_recv, back_send, back_recv, out_send, out_recv,
-    doc_lengths, doc_sem,
+    doc_lengths, doc_sem, met,
 ):
     me = lax.axis_index("blk")
     group, rank = me // RING, lax.rem(me, RING)
@@ -143,17 +143,21 @@
     for k in range(1, RING):
         pl.semaphore_signal(barrier, inc=1, device_id=ring_device(member(k)), device_id_type=MESH)
 
-    @pl.when(has_next)
-    def _():
-        pl.semaphore_signal(barrier, inc=1, device_id=next_device, device_id_type=MESH)
-
-    @pl.when(has_prev)
-    def _():
-        pl.semaphore_signal(barrier, inc=1, device_id=prev_device, device_id_type=MESH)
-
+    even = lax.rem(group, 2) == 0
+    neighbours = has_next.astype(jnp.int32) + has_prev.astype(jnp.int32)
+
+    def greet(semaphore, when):
+        for present, device in ((has_next, next_device), (has_prev, prev_device)):
+
+            @pl.when(present & when)
+            def _():
+                pl.semaphore_signal(semaphore, inc=1, device_id=device, device_id_type=MESH)
+
+    greet(barrier, even)
     doc_copy = pltpu.make_async_copy(doc_lengths_in, doc_lengths, doc_sem)
     doc_copy.start()
-    pl.semaphore_wait(barrier, RING - 1 + has_next.astype(jnp.int32) + has_prev.astype(jnp.int32))
+    pl.semaphore_wait(barrier, RING - 1 + jnp.where(even, 0, neighbours))
+    greet(met, jnp.logical_not(even))
 
     sends = [(hh, a, k) for hh in range(HEADS_EACH) for a in (0, 2) for k in range(1, RING)]
     paced = (2 * HEADS_EACH - 1) * (RING - 1)
@@ -195,6 +199,10 @@
         first_key = jnp.where(position >= doc_end, doc_end, first_key)
     window_base = group * RING * tok - halo + lax.broadcasted_iota(jnp.int32, (RING, tok), 0) * tok
     start_ref[...] = first_key - window_base
+
+    @pl.when(even)
+    def _():
+        pl.semaphore_wait(met, neighbours)
 
     forward(0, rank)
 
@@ -305,7 +313,7 @@
         @pl.when(i == RING - 1)
         def _():
             def finish(k, _):
-                shard = member(k)
+                shard = k
 
                 def put(dk, dv):
                     stage[hh, 2, rows(shard), :] = dk.astype(jnp.bfloat16)
@@ -418,6 +426,7 @@
                 dma((2,)),
                 pltpu.SMEM(doc_lengths.shape, jnp.int32),
                 dma(()),
+                pltpu.SemaphoreType.REGULAR,
             ],
             compiler_params=pltpu.CompilerParams(
                 collective_id=0, has_side_effects=True, vmem_limit_bytes=58 * 2**20

time: 103 us -> 101 us (0.981)
    pallas_call x1, Pallas kernels: 99.8 us -> 98.7 us  [on_device(): pl.pallas_call(functools.partial(kernel, n_blk, tok), out_shape=landing,...]
where the time goes in v5:
time: 101 us
  Pallas kernels  101 us (100%)
    pallas_call x1, Pallas kernels, on_device(): pl.pallas_call(functools.partial(kernel, n_blk, tok), out_shape=landing,...  98.7 us
    pallas_call x1, Pallas kernels, on_device(): pl.pallas_call(write_out, out_shape=[out] * 4, in_specs=[any_space], out_...  2.04 us

profile of v5, /device:TPU:1, one launch (start us, length us, event | category | flops | bytes accessed | tf_op | source)
XLA Modules:
  0.0 101.4 jit_solution(13839057653327774224)
XLA Ops:
  0.6 98.7 %shard_map.84.landing = bf16[4,256,2048]{2,1,0:T(8,128)(2,1)S(1)} custom-call(s32[16]{0:T(128)} %doc_lengths_in.1, bf16[256,2048]{1,0:T(8,128)(2,1)} %q_in.1, bf16[256,2048]{1,0:T(8,128)(2,1)} %k_in.1, bf16[256,2048]{1,0:T(8,128)(2,1)} %v_in.1, bf16[256,2048]{1,0:T(8,128)(2,1)} %g_in.1), custom_call_target="tpu_custom_call" | custom-call | flops 11274289152 | bytes 8388608 | tf_op jit(solution)/shard_map/pallas_call | solution.py:397
  99.3 2.0 %shard_map.85 = (bf16[256,2048]{1,0:T(8,128)(2,1)}, bf16[256,2048]{1,0:T(8,128)(2,1)}, bf16[256,2048]{1,0:T(8,128)(2,1)}, bf16[256,2048]{1,0:T(8,128)(2,1)}) custom-call(bf16[4,256,2048]{2,1,0:T(8,128)(2,1)S(1)} %shard_map.84.landing), custom_call_target="tpu_custom_call" | custom-call | bytes 8388608 | tf_op jit(solution)/shard_map/pallas_call | solution.py:438

commit v6 on v5

--- a/solution.py
+++ b/solution.py
@@ -310,39 +310,42 @@
             for a in range(2):
                 back_copy(hh, a, i).start()
 
+        def finish(shard, _):
+
+            def put(dk, dv):
+                stage[hh, 2, rows(shard), :] = dk.astype(jnp.bfloat16)
+                stage[hh, 3, rows(shard), :] = dv.astype(jnp.bfloat16)
+
+            own = rows(shard + REACH)
+
+            @pl.when(shard < RING - REACH)
+            def _():
+                put(acc_k[own, :] * SCALE, acc_v[own, :])
+
+            @pl.when(shard >= RING - REACH)
+            def _():
+                h = shard - (RING - REACH)
+
+                @pl.when(has_next)
+                def _():
+                    for a in range(2):
+                        landed(halo_recv.at[hh, a, rows(h), :], back_recv.at[hh, a, h])
+
+                put(
+                    acc_k[own, :] * SCALE + halo_recv[hh, 0, rows(h), :].astype(jnp.float32),
+                    acc_v[own, :] + halo_recv[hh, 1, rows(h), :].astype(jnp.float32),
+                )
+
+            send_results(hh, 2, shard)
+            return 0
+
+        @pl.when(i == RING - 2)
+        def _():
+            finish(jnp.int32(0), 0)
+
         @pl.when(i == RING - 1)
         def _():
-            def finish(k, _):
-                shard = k
-
-                def put(dk, dv):
-                    stage[hh, 2, rows(shard), :] = dk.astype(jnp.bfloat16)
-                    stage[hh, 3, rows(shard), :] = dv.astype(jnp.bfloat16)
-
-                own = rows(shard + REACH)
-
-                @pl.when(shard < RING - REACH)
-                def _():
-                    put(acc_k[own, :] * SCALE, acc_v[own, :])
-
-                @pl.when(shard >= RING - REACH)
-                def _():
-                    h = shard - (RING - REACH)
-
-                    @pl.when(has_next)
-                    def _():
-                        for a in range(2):
-                            landed(halo_recv.at[hh, a, rows(h), :], back_recv.at[hh, a, h])
-
-                    put(
-                        acc_k[own, :] * SCALE + halo_recv[hh, 0, rows(h), :].astype(jnp.float32),
-                        acc_v[own, :] + halo_recv[hh, 1, rows(h), :].astype(jnp.float32),
-                    )
-
-                send_results(hh, 2, shard)
-                return 0
-
-            lax.fori_loop(0, RING, finish, 0)
+            lax.fori_loop(1, RING, finish, 0)
 
         return 0
 

time: 101 us -> 101 us (level)
  no operation moved by 1% of the time
where the time goes in v6:
time: 101 us
  Pallas kernels  101 us (100%)
    pallas_call x1, Pallas kernels, on_device(): pl.pallas_call(functools.partial(kernel, n_blk, tok), out_shape=landing,...  98.7 us
    pallas_call x1, Pallas kernels, on_device(): pl.pallas_call(write_out, out_shape=[out] * 4, in_specs=[any_space], out_...  2.04 us

profile of v6, /device:TPU:1, one launch (start us, length us, event | category | flops | bytes accessed | tf_op | source)
XLA Modules:
  0.0 101.4 jit_solution(3625800865703458817)
XLA Ops:
  0.6 98.7 %shard_map.84.landing = bf16[4,256,2048]{2,1,0:T(8,128)(2,1)S(1)} custom-call(s32[16]{0:T(128)} %doc_lengths_in.1, bf16[256,2048]{1,0:T(8,128)(2,1)} %q_in.1, bf16[256,2048]{1,0:T(8,128)(2,1)} %k_in.1, bf16[256,2048]{1,0:T(8,128)(2,1)} %v_in.1, bf16[256,2048]{1,0:T(8,128)(2,1)} %g_in.1), custom_call_target="tpu_custom_call" | custom-call | flops 11274289152 | bytes 8388608 | tf_op jit(solution)/shard_map/pallas_call | solution.py:400
  99.3 2.0 %shard_map.85 = (bf16[256,2048]{1,0:T(8,128)(2,1)}, bf16[256,2048]{1,0:T(8,128)(2,1)}, bf16[256,2048]{1,0:T(8,128)(2,1)}, bf16[256,2048]{1,0:T(8,128)(2,1)}) custom-call(bf16[4,256,2048]{2,1,0:T(8,128)(2,1)S(1)} %shard_map.84.landing), custom_call_target="tpu_custom_call" | custom-call | bytes 8388608 | tf_op jit(solution)/shard_map/pallas_call | solution.py:441

commit v7 on v5

--- a/solution.py
+++ b/solution.py
@@ -13,6 +13,7 @@
 RING = 8
 HEADS_EACH = 2
 WINDOW = 12
+DISTANCES = (2, 6, 1, 3, 7, 5, 4)
 NEG_FILL = -1e30
 SCALE = 1.0 / math.sqrt(HEAD_DIM)
 SCALE_LOG2 = SCALE * math.log2(math.e)
@@ -159,7 +160,7 @@
     pl.semaphore_wait(barrier, RING - 1 + jnp.where(even, 0, neighbours))
     greet(met, jnp.logical_not(even))
 
-    sends = [(hh, a, k) for hh in range(HEADS_EACH) for a in (0, 2) for k in range(1, RING)]
+    sends = [(hh, a, k) for hh in range(HEADS_EACH) for a in (0, 2) for k in DISTANCES]
     paced = (2 * HEADS_EACH - 1) * (RING - 1)
 
     def start_send(n):
@@ -210,7 +211,7 @@
         wait_send(n - WINDOW)
         start_send(n)
         if n - WINDOW < RING - 1:
-            forward(0, member(-(n - WINDOW + 1)))
+            forward(0, member(-sends[n - WINDOW][2]))
     forward(1, rank)
 
     def transposed(hh, shard):

time: 101 us -> 101 us (level)
  no operation moved by 1% of the time
where the time goes in v7:
time: 101 us
  Pallas kernels  101 us (100%)
    pallas_call x1, Pallas kernels, on_device(): pl.pallas_call(functools.partial(kernel, n_blk, tok), out_shape=landing,...  98.7 us
    pallas_call x1, Pallas kernels, on_device(): pl.pallas_call(write_out, out_shape=[out] * 4, in_specs=[any_space], out_...  2.04 us

profile of v7, /device:TPU:1, one launch (start us, length us, event | category | flops | bytes accessed | tf_op | source)
XLA Modules:
  0.0 101.4 jit_solution(6739789738382390362)
XLA Ops:
  0.6 98.7 %shard_map.84.landing = bf16[4,256,2048]{2,1,0:T(8,128)(2,1)S(1)} custom-call(s32[16]{0:T(128)} %doc_lengths_in.1, bf16[256,2048]{1,0:T(8,128)(2,1)} %q_in.1, bf16[256,2048]{1,0:T(8,128)(2,1)} %k_in.1, bf16[256,2048]{1,0:T(8,128)(2,1)} %v_in.1, bf16[256,2048]{1,0:T(8,128)(2,1)} %g_in.1), custom_call_target="tpu_custom_call" | custom-call | flops 11274289152 | bytes 8388608 | tf_op jit(solution)/shard_map/pallas_call | solution.py:398
  99.3 2.0 %shard_map.85 = (bf16[256,2048]{1,0:T(8,128)(2,1)}, bf16[256,2048]{1,0:T(8,128)(2,1)}, bf16[256,2048]{1,0:T(8,128)(2,1)}, bf16[256,2048]{1,0:T(8,128)(2,1)}) custom-call(bf16[4,256,2048]{2,1,0:T(8,128)(2,1)S(1)} %shard_map.84.landing), custom_call_target="tpu_custom_call" | custom-call | bytes 8388608 | tf_op jit(solution)/shard_map/pallas_call | solution.py:439
